TPU v7x, 256 devices: a whole 4x4x8 slice. The times are simulated.
256 devices in a mesh: dp: 32 (over y, x, core), mp: 8 (over z).
Axes of the slice: x: 4, y: 4, z: 8, core: 2. Of those that a mesh axis runs over, the one named last changes fastest.
Arguments:
- acts: bfloat16 [128, 256, 18432], P('dp', None, 'mp'), may hold values from -60 to 60
- out_grads: bfloat16 [128, 256, 2304], P('dp', None, 'mp'), may hold values from -60 to 60
Outputs:
- grad_mean: float32 [2304, 18432], P('dp', 'mp')
- clip_factor: float32 [128], P('dp')
All inputs are finite; a program needn't handle non-finite values.
Results may differ from a plain program's by a relative error of at most 0.002.
Values may be sent and summed in bfloat16 or wider, within the bound.
A program may use at most 128 MiB of HBM per device.

v0:
```python
import math

import jax
import jax.numpy as jnp
from jax import lax
from jax.sharding import PartitionSpec as P

D = 2304
F = 18432
SEQ = 256


def on_device(acts, out_grads):
    count_ex, seq_len, local_hidden = acts.shape
    data_devices = lax.axis_size("dp")
    bound = math.sqrt(F * D * SEQ)
    whole = lax.all_gather(out_grads, "mp", axis=2, tiled=True)
    full_width = whole.shape[2]
    act_gram = jnp.einsum("btf,bsf->bts", acts, acts, preferred_element_type=jnp.float32)
    grad_gram = jnp.einsum("btd,bsd->bts", whole, whole, preferred_element_type=jnp.float32)
    summed_gram = lax.psum(act_gram, "mp")
    sq_norm = jnp.sum(summed_gram * grad_gram, axis=(1, 2))
    clip_factor = bound / jnp.maximum(jnp.sqrt(sq_norm), bound)
    scaled = (whole.astype(jnp.float32) * clip_factor[:, None, None]).astype(jnp.bfloat16)
    flat_acts = acts.reshape(count_ex * seq_len, local_hidden)
    flat_grads = scaled.reshape(count_ex * seq_len, full_width)
    contract = (((0,), (0,)), ((), ()))
    summed = lax.psum_scatter(
        lax.dot_general(flat_grads, flat_acts, contract, preferred_element_type=jnp.float32),
        "dp",
        scatter_dimension=0,
        tiled=True,
    )
    return (summed / (count_ex * data_devices), clip_factor)


def solution(mesh):
    in_specs = (P("dp", None, "mp"), P("dp", None, "mp"))
    out_specs = (P("dp", "mp"), P("dp"))
    return jax.shard_map(
        on_device, mesh=mesh, in_specs=in_specs, out_specs=out_specs, check_vma=False
    )
```

profile of v0, /device:TPU:2, one launch (start us, length us, event | category | flops | bytes accessed | tf_op | source)
XLA Modules:
  0.0 320.6 jit_solution(13280045920444811843)
XLA Ops:
  7.2 0.0 all-reduce.2.cloned.1.call-start
  7.2 6.2 %fusion.2 = f32[4,256,256]{2,1,0:T(8,128)} fusion(bf16[4,256,2304]{2,1,0:T(8,128)(2,1)} %param.2), kind=kOutput, calls=%fused_computation.7 | convolution fusion | flops 1207959552 | bytes 5767168 | tf_op jit(solution)/shard_map/btf,bsf->bts/dot_general | solution.py:19
  13.4 0.0 all-reduce.2.cloned.1.call-update
  13.4 0.0 all-gather.2.cloned.1.call-start
  13.5 0.7 all-gather.2.cloned.1.call-update
  14.2 0.0 reduce-scatter.2.cloned.1.call-start
  14.2 78.3 %all-reduce.2.cloned.1.call-done = f32[4,256,256]{2,1,0:T(8,128)} async-done(((f32[4,256,256]{2,1,0:T(8,128)}), f32[4,256,256]{2,1,0:T(8,128)}) %all-reduce.2.cloned.1.call-update) | async-done | bytes 1048592 | tf_op jit(solution)/shard_map/psum | solution.py:21
  92.5 60.0 %all-gather.2.cloned.1.call-done = bf16[4,256,2304]{1,2,0:T(8,128)(2,1)} async-done(((bf16[4,256,288]{1,2,0:T(8,128)(2,1)}), bf16[4,256,2304]{1,2,0:T(8,128)(2,1)}) %all-gather.2.cloned.1.call-update) | async-done | bytes 4718608 | tf_op jit(solution)/shard_map/all_gather | solution.py:17
  152.5 0.0 copy-start
  152.5 5.9 %fusion.1 = f32[4]{0:T(128)S(1)} fusion(f32[4,256,256]{2,1,0:T(8,128)} %all-reduce.2.cloned.1.call-done, bf16[4,256,2304]{1,2,0:T(8,128)(2,1)} %all-gather.2.cloned.1.call-done), kind=kOutput, calls=%fused_computation.4 | convolution fusion | flops 1208483840 | bytes 5767184 | tf_op jit(solution)/shard_map/btd,bsd->bts/dot_general | solution.py:20
  158.5 0.0 copy-done
  158.5 0.0 copy-start.1
  158.5 18.4 %convolution_bitcast_fusion = f32[2304,2304]{1,0:T(8,128)} fusion(bf16[4,256,2304]{2,1,0:T(8,128)(2,1)} %param.2, bf16[4,256,2304]{1,2,0:T(8,128)(2,1)S(1)} %copy-done, f32[4]{0:T(128)S(1)} %maximum_divide_fusion), kind=kOutput, calls=%fused_computation | convolution fusion | flops 10878713856 | bytes 30670864 | tf_op jit(solution)/shard_map/dot_general | solution.py:29
  176.9 0.0 copy-done.1
  176.9 0.0 reduce-scatter.2.cloned.1.call-update
  176.9 135.1 %reduce-scatter.2.cloned.1.call-done = f32[72,2304]{1,0:T(8,128)} async-done(((f32[2304,2304]{1,0:T(8,128)}), f32[72,2304]{1,0:T(8,128)}) %reduce-scatter.2.cloned.1.call-update) | async-done | bytes 663568 | tf_op jit(solution)/shard_map/reduce_scatter | solution.py:28
  312.0 2.0 broadcast_multiply_fusion
  (1 shorter events, 0.0 us)
Async XLA Ops:
  7.2 85.3 %all-reduce.2.cloned.1.call-start = ((), (), s32[]{:S(2)}) async-start(), calls=%async_computation.2 | async-start | bytes 2097152 | tf_op jit(solution)/shard_map/psum | solution.py:21
  13.4 139.1 %all-gather.2.cloned.1.call-start = ((), (), s32[]{:S(2)}) async-start(), calls=%async_computation.1 | async-start | bytes 5308416 | tf_op jit(solution)/shard_map/all_gather | solution.py:17
  14.2 297.9 %reduce-scatter.2.cloned.1.call-start = ((), (), s32[]{:S(2)}) async-start(), calls=%async_computation.3 | async-start | bytes 21897216 | tf_op jit(solution)/shard_map/reduce_scatter | solution.py:28
  152.5 6.0 %copy-start = (bf16[4,256,2304]{1,2,0:T(8,128)(2,1)S(1)}, bf16[4,256,2304]{1,2,0:T(8,128)(2,1)}, u32[]{:S(2)}) copy-start(bf16[4,256,2304]{1,2,0:T(8,128)(2,1)} %all-gather.2.cloned.1.call-done) | copy-start | bytes 14155780
  158.5 18.4 %copy-start.1 = (f32[4]{0:T(128)}, f32[4]{0:T(128)S(1)}, u32[]{:S(2)}) copy-start(f32[4]{0:T(128)S(1)} %maximum_divide_fusion) | copy-start | bytes 52
Sparse Core Ops, SparseCore 0:
  13.5 78.9 all-reduce.1
  94.3 58.2 all-gather.1
  177.0 134.9 reduce-scatter.1
where the time goes:
time: 321 us
  waiting for transfers between devices  274 us (85%)
  matrix products  30.5 us (10%)
  between operations  13.8 us (4%)
    reduce_scatter x1, waiting for transfers between devices, on_device(): lax.psum_scatter(lax.dot_general(flat_grads, flat_acts, contract, preferr...  135 us
    psum x1, waiting for transfers between devices, on_device(): summed_gram = lax.psum(act_gram, 'mp')  78.3 us
    all_gather x1, waiting for transfers between devices, on_device(): whole = lax.all_gather(out_grads, 'mp', axis=2, tiled=True)  60 us
    dot_general x1, matrix products, on_device(): lax.dot_general(flat_grads, flat_acts, contract, preferred_element_type=j...  18.4 us
  transfers between devices with their start and end apart: 3, of which 3 were waited for; matrix products, arithmetic and copies ran while one was open for 0% of the time, Pallas kernels for 0%

commit v1 on v0

v1 whole, which is shorter than its diff:
```python
import functools
import math

import jax
import jax.numpy as jnp
from jax import lax
from jax.experimental import pallas as pl
from jax.experimental.pallas import tpu as pltpu
from jax.sharding import PartitionSpec as P

D = 2304
F = 18432
SEQ = 256
MESH = pl.DeviceIdType.MESH
NZ = 8
SIDE = 4
OWN = 72
EX = 4
TOK = EX * SEQ
COLS = F // NZ
BOUND = math.sqrt(F * D * SEQ)
PIECES = ((0, 32, 1280), (32, 24, 1024), (56, 16, 1280))
TILE = 256
F32, BF16 = jnp.float32, jnp.bfloat16


def tn_dot(a, b):
    return lax.dot_general(a, b, (((0,), (0,)), ((), ())), preferred_element_type=F32)


def nt_dot(a, b):
    return lax.dot_general(a, b, (((1,), (1,)), ((), ())), preferred_element_type=F32)


def kernel(x_hbm, g_hbm, out, clip_out, *scratch):
    names = iter(scratch)
    acts, graw, gt, clipv, tile, parts, agram, ggram = (next(names) for _ in range(8))
    grads = [next(names) for _ in PIECES]
    peer = [next(names) for _ in PIECES]
    scaled = [next(names) for _ in PIECES]
    part = [next(names) for _ in PIECES]
    send1 = [(next(names), next(names)) for _ in PIECES]
    recv1 = [(next(names), next(names)) for _ in PIECES]
    sums = [(next(names), next(names)) for _ in PIECES]
    recv2 = [(next(names), next(names)) for _ in PIECES]
    local_sem, pair_s, pair_r, ring_s, ring_r, norm_s, norm_r, p1_s, p1_r, p2_s, p2_r = names

    dp, z = lax.axis_index("dp"), lax.axis_index("mp")
    y, x, c = dp // 8, (dp // 2) % SIDE, dp % 2
    other = 1 - c

    def at(y, x, c, z):
        return (y * 8 + x * 2 + c, z)

    def xs(k):
        return lax.rem(x + k, SIDE)

    def ys(k):
        return lax.rem(y + k, SIDE)

    def zs(k):
        return lax.rem(z + k + NZ, NZ)

    peer_id = at(y, x, other, z)
    group = [(dz, dc) for dz in range(NZ) for dc in range(2) if dz or dc]

    def group_id(dz, dc):
        return at(y, x, lax.rem(c + dc, 2), zs(dz))

    load_x = pltpu.make_async_copy(x_hbm, acts.at[pl.ds(c * EX, EX)], local_sem.at[0])
    load_g = pltpu.make_async_copy(g_hbm, graw, local_sem.at[1])
    load_g.start()
    load_x.start()

    barrier = pltpu.get_barrier_semaphore()
    for dz, dc in group:
        pl.semaphore_signal(barrier, inc=1, device_id=group_id(dz, dc), device_id_type=MESH)
    for k in range(1, SIDE):
        pl.semaphore_signal(barrier, inc=1, device_id=at(y, xs(k), c, z), device_id_type=MESH)
        pl.semaphore_signal(barrier, inc=1, device_id=at(ys(k), x, c, z), device_id_type=MESH)
    pl.semaphore_wait(barrier, len(group) + 2 * (SIDE - 1))

    def remote(src, dst, ssem, rsem, to):
        return pltpu.make_async_remote_copy(
            src_ref=src, dst_ref=dst, send_sem=ssem, recv_sem=rsem, device_id=to, device_id_type=MESH
        )

    def pair_x():
        here = acts.at[pl.ds(c * EX, EX)]
        return remote(x_hbm, here, pair_s.at[0], pair_r.at[0], peer_id)

    pair_x().start()

    load_g.wait()
    for e in range(EX):
        gt[:, e * SEQ:(e + 1) * SEQ] = graw[e].astype(F32).T
    token0 = pl.multiple_of(c * TOK, TOK)
    token1 = pl.multiple_of(other * TOK, TOK)

    def rows_of(core, first, n):
        return jnp.concatenate(
            [gt[pl.ds(pl.multiple_of(a * 2 * OWN + core * OWN + first, 8), n), :] for a in range(2)], axis=0
        ).astype(BF16)

    def pair_g(p):
        return remote(peer[p], grads[p].at[z, :, pl.ds(token0, TOK)], pair_s.at[1 + p], pair_r.at[1 + p], peer_id)

    for p, (first, n, _) in enumerate(PIECES):
        peer[p][...] = rows_of(other, first, n)
        pair_g(p).start()
        grads[p][z, :, pl.ds(token0, TOK)] = rows_of(c, first, n)

    def ring(p, s, h, q):
        src = zs(-(h - 1) if s == 0 else h - 1)
        view = grads[p].at[src, :, pl.ds(token0 if q == 0 else token1, TOK)]
        return remote(view, view, ring_s.at[p, s, h - 1, q], ring_r.at[p, s, h - 1, q],
                      at(y, x, c, zs(1 if s == 0 else -1)))

    def ring_in(p, s, h, q):
        src = zs(-h if s == 0 else h)
        view = grads[p].at[src, :, pl.ds(token0 if q == 0 else token1, TOK)]
        return remote(view, view, ring_s.at[p, s, h - 1, q], ring_r.at[p, s, h - 1, q],
                      at(y, x, c, zs(1 if s == 0 else -1)))

    def wait_pair_g(p):
        view = grads[p].at[z, :, pl.ds(token1, TOK)]
        remote(peer[p], view, pair_s.at[1 + p], pair_r.at[1 + p], peer_id).wait_recv()

    def ring_step(p, h):
        for q in range(2):
            if h == 1 and q == 1:
                wait_pair_g(p)
            for s in range(2):
                if h == 4 and s != q:
                    continue
                if h > 1:
                    ring_in(p, s, h - 1, q).wait_recv()
                ring(p, s, h, q).start()
        if h == 4:
            for s in range(2):
                ring_in(p, s, 3, 1 - s).wait_recv()

    def ring_last(p):
        for s in range(2):
            ring_in(p, s, 4, s).wait_recv()

    def act_gram(b):
        agram[b] = nt_dot(acts[b], acts[b])

    def grad_gram(p):
        n = PIECES[p][1]

        def body(b, _):
            cols = pl.ds(pl.multiple_of(b * SEQ, SEQ), SEQ)
            v = grads[p][:, :, cols].reshape(NZ * 2 * n, SEQ)
            g = tn_dot(v, v)
            ggram[b] = g if p == 0 else ggram[b] + g
            return 0

        lax.fori_loop(0, 2 * EX, body, 0)

    NP = len(PIECES)
    for p in range(NP):
        for h in range(1, 5):
            ring_step(p, h)
            if p == 0 and h == 2:
                load_x.wait()
                remote(x_hbm, acts.at[pl.ds(other * EX, EX)], pair_s.at[0], pair_r.at[0], peer_id).wait_recv()
            if p == 0 and h >= 3 or p == 1:
                i = (p * 4 + h - 3)
                if i < 4:
                    act_gram(2 * i)
                    act_gram(2 * i + 1)
            if p and h == 1:
                ring_last(p - 1)
                grad_gram(p - 1)
    ring_last(NP - 1)
    grad_gram(NP - 1)

    for b in range(2 * EX):
        v = jnp.sum(agram[b] * ggram[b], axis=0, keepdims=True)
        tile[b:b + 1, :] = v[:, :128] + v[:, 128:]
    slot = z * 2 + c
    parts[slot] = tile[...]

    def norm(i):
        dz, dc = group[i]
        return remote(tile, parts.at[slot], norm_s.at[i], norm_r.at[i], group_id(dz, dc))

    def norm_in(i):
        dz, dc = group[i]
        src = lax.rem(z - dz + NZ, NZ) * 2 + lax.rem(c + dc, 2)
        return remote(tile, parts.at[src], norm_s.at[i], norm_r.at[i], group_id(dz, dc))

    for i in range(len(group)):
        norm(i).start()
    for i in range(len(group)):
        norm_in(i).wait_recv()
    total = jnp.sum(jnp.sum(parts[...], axis=0), axis=1, keepdims=True)
    factor = BOUND / jnp.maximum(jnp.sqrt(total), BOUND)
    for b in range(2 * EX):
        clipv[:, b * SEQ:(b + 1) * SEQ] = jnp.broadcast_to(factor[b:b + 1, :], (1, SEQ))
    for e in range(EX):
        v = clipv[:, pl.ds(pl.multiple_of((c * EX + e) * SEQ, SEQ), 128)]
        clip_out[e] = jnp.max(v)

    def p1(p, half, k):
        to = at(y, xs(k), c, z) if half == 0 else at(ys(k), x, c, z)
        return remote(send1[p][half].at[k - 1], recv1[p][half].at[k - 1],
                      p1_s.at[p, half, k - 1], p1_r.at[p, half, k - 1], to)

    def p2(p, half, k):
        to = at(ys(k), x, c, z) if half == 0 else at(y, xs(k), c, z)
        block = ys(k) if half == 0 else xs(k)
        return remote(sums[p][half].at[block], recv2[p][half].at[k - 1],
                      p2_s.at[p, half, k - 1], p2_r.at[p, half, k - 1], to)

    def span(p, half):
        cut = PIECES[p][2]
        return (0, cut) if half == 0 else (cut, COLS - cut)

    def dests(half, k):
        if half == 0:
            return [i * SIDE + xs(k) for i in range(SIDE)]
        return [ys(k) * SIDE + i for i in range(SIDE)]

    def multiply(p):
        first, n, _ = PIECES[p]
        for zz in range(NZ):
            scaled[p][zz] = (grads[p][zz].astype(F32) * clipv[...]).astype(BF16)
        for half in range(2):
            base, width = span(p, half)

            def body(i, _):
                cols = pl.ds(pl.multiple_of(base + i * TILE, TILE), TILE)
                local = pl.ds(pl.multiple_of(i * TILE, TILE), TILE)
                lhs = scaled[p][...].reshape(NZ * 2 * n, 2 * TOK)
                rhs = acts[:, :, cols].reshape(2 * TOK, TILE)
                part[p][:, :, cols] = jnp.dot(lhs, rhs, preferred_element_type=F32).reshape(16, n, TILE)
                for k in range(1, SIDE):
                    v = jnp.concatenate([part[p][j, :, cols] for j in dests(half, k)], axis=0)
                    send1[p][half][k - 1, :, local] = v.astype(BF16)
                return 0

            lax.fori_loop(0, width // TILE, body, 0)
            for k in range(1, SIDE):
                p1(p, half, k).start()

    def reduce1(p, half):
        first, n, _ = PIECES[p]
        base, width = span(p, half)
        for k in range(1, SIDE):
            p1(p, half, k).wait_recv()

        def body(i, _):
            cols = pl.ds(pl.multiple_of(base + i * TILE, TILE), TILE)
            local = pl.ds(pl.multiple_of(i * TILE, TILE), TILE)
            v = jnp.concatenate([part[p][j, :, cols] for j in dests(half, 0)], axis=0)
            for k in range(1, SIDE):
                v = v + recv1[p][half][k - 1, :, local].astype(F32)
            for i in range(SIDE):
                sums[p][half][i, :, local] = v[i * n:(i + 1) * n]
            return 0

        lax.fori_loop(0, width // TILE, body, 0)
        for k in range(1, SIDE):
            p2(p, half, k).start()

    def reduce2(p, half):
        first, n, _ = PIECES[p]
        base, width = span(p, half)
        for k in range(1, SIDE):
            p2(p, half, k).wait_recv()
        v = sums[p][half][y if half == 0 else x]
        for k in range(1, SIDE):
            v = v + recv2[p][half][k - 1]
        out[first:first + n, base:base + width] = v * (1.0 / 128)

    for p in range(NP):
        multiply(p)
        if p:
            for half in range(2):
                reduce1(p - 1, half)
    for half in range(2):
        reduce1(NP - 1, half)
    for p in range(NP):
        for half in range(2):
            reduce2(p, half)

    pair_x().wait_send()
    for p in range(NP):
        pair_g(p).wait_send()
        for s in range(2):
            for h in range(1, 5):
                for q in range(2):
                    if h < 4 or s == q:
                        ring(p, s, h, q).wait_send()
        for half in range(2):
            for k in range(1, SIDE):
                p1(p, half, k).wait_send()
                p2(p, half, k).wait_send()
    for i in range(len(group)):
        norm(i).wait_send()


def on_device(acts, out_grads):
    np_ = len(PIECES)
    dma = pltpu.SemaphoreType.DMA
    scratch = [
        pltpu.VMEM((2 * EX, SEQ, COLS), BF16),
        pltpu.VMEM((EX, SEQ, D // NZ), BF16),
        pltpu.VMEM((D // NZ, TOK), F32),
        pltpu.VMEM((1, 2 * TOK), F32),
        pltpu.VMEM((2 * EX, 128), F32),
        pltpu.VMEM((2 * NZ, 2 * EX, 128), F32),
        pltpu.VMEM((2 * EX, SEQ, SEQ), F32),
        pltpu.VMEM((2 * EX, SEQ, SEQ), F32),
    ]
    widths = [((0, cut), (1, COLS - cut)) for _, _, cut in PIECES]
    scratch += [pltpu.VMEM((NZ, 2 * n, 2 * TOK), BF16) for _, n, _ in PIECES]
    scratch += [pltpu.VMEM((2 * n, TOK), BF16) for _, n, _ in PIECES]
    scratch += [pltpu.VMEM((NZ, 2 * n, 2 * TOK), BF16) for _, n, _ in PIECES]
    scratch += [pltpu.VMEM((16, n, COLS), F32) for _, n, _ in PIECES]
    for shape in ("send", "recv"):
        scratch += [
            pltpu.VMEM((3, 4 * n, w), BF16) for (_, n, cut) in PIECES for w in (cut, COLS - cut)
        ]
    scratch += [pltpu.VMEM((4, n, w), F32) for (_, n, cut) in PIECES for w in (cut, COLS - cut)]
    scratch += [pltpu.VMEM((3, n, w), F32) for (_, n, cut) in PIECES for w in (cut, COLS - cut)]
    scratch += [
        dma((2,)),
        dma((1 + np_,)),
        dma((1 + np_,)),
        dma((np_, 2, 4, 2)),
        dma((np_, 2, 4, 2)),
        dma((15,)),
        dma((15,)),
        dma((np_, 2, 3)),
        dma((np_, 2, 3)),
        dma((np_, 2, 3)),
        dma((np_, 2, 3)),
    ]
    return pl.pallas_call(
        kernel,
        out_shape=(
            jax.ShapeDtypeStruct((OWN, COLS), F32),
            jax.ShapeDtypeStruct((EX,), F32),
        ),
        in_specs=[pl.BlockSpec(memory_space=pl.ANY)] * 2,
        out_specs=(pl.BlockSpec(memory_space=pltpu.VMEM), pl.BlockSpec(memory_space=pltpu.SMEM)),
        scratch_shapes=scratch,
        compiler_params=pltpu.CompilerParams(
            collective_id=0, has_side_effects=True, vmem_limit_bytes=60 * 2**20
        ),
        name="clipped_grad",
    )(acts, out_grads)


def solution(mesh):
    in_specs = (P("dp", None, "mp"), P("dp", None, "mp"))
    out_specs = (P("dp", "mp"), P("dp"))
    return jax.shard_map(
        on_device, mesh=mesh, in_specs=in_specs, out_specs=out_specs, check_vma=False
    )
```

time: 321 us -> 135 us (0.42)
  waiting for transfers between devices: 274 us -> 0 us
  Pallas kernels: 0 us -> 129 us
  matrix products: 30.5 us -> 0 us
  between operations: 13.8 us -> 0.64 us
  local copies, waits for them, and re-layouts: 0.01 us -> 5.32 us
    reduce_scatter x1 -> x0, waiting for transfers between devices: 135 us -> none  [on_device(): lax.psum_scatter(lax.dot_general(flat_grads, flat_acts, contract, preferr...]
    pallas_call x0 -> x1, Pallas kernels: none -> 129 us  [on_device(): pl.pallas_call(kernel, out_shape=(jax.ShapeDtypeStruct((OWN, COLS), F32),...]
    psum x1 -> x0, waiting for transfers between devices: 78.3 us -> none  [on_device(): summed_gram = lax.psum(act_gram, 'mp')]
    all_gather x1 -> x0, waiting for transfers between devices: 60 us -> none  [on_device(): whole = lax.all_gather(out_grads, 'mp', axis=2, tiled=True)]
    dot_general x3 -> x0, matrix products: 30.5 us -> none  [the longest x1 18.4 us: on_device(): lax.dot_general(flat_grads, flat_acts, contract, preferred_element_type=j...]
    unnamed x4 -> x3, local copies, waits for them, and re-layouts: 0.01 us -> 5.32 us
  transfers between devices with their start and end apart: 3 -> 0, of which waited for: 3 -> 0; matrix products, arithmetic and copies ran while one was open for 0% -> 0% of each run, Pallas kernels for 0% -> 0%
where the time goes in v1:
time: 135 us
  Pallas kernels  129 us (96%)
  local copies, waits for them, and re-layouts  5.32 us (4%)
    pallas_call x1, Pallas kernels, on_device(): pl.pallas_call(kernel, out_shape=(jax.ShapeDtypeStruct((OWN, COLS), F32),...  129 us
    unnamed x3, local copies, waits for them, and re-layouts  5.32 us

profile of v1, /device:TPU:2, one launch (start us, length us, event | category | flops | bytes accessed | tf_op | source)
XLA Modules:
  0.0 134.5 jit_solution(9823821570731172835)
XLA Ops:
  0.6 2.2 %copy.4.g_hbm = bf16[4,256,288]{2,1,0:T(8,128)(2,1)} copy(bf16[4,256,288]{1,2,0:T(8,128)(2,1)} %param.3) | data formatting | bytes 1179648 | tf_op args[1]
  2.9 128.5 %clipped_grad.1 = (f32[72,2304]{1,0:T(8,128)}, f32[4]{0:T(128)}) custom-call(bf16[4,256,2304]{2,1,0:T(8,128)(2,1)} %x_hbm.1, bf16[4,256,288]{2,1,0:T(8,128)(2,1)} %copy.4.g_hbm), custom_call_target="tpu_custom_call" | custom-call | tf_op jit(solution)/shard_map/clipped_grad/pallas_call | solution.py:343
  131.4 2.0 %copy.7 = f32[72,2304]{1,0:T(8,128)} copy(f32[72,2304]{1,0:T(8,128)} %get-tuple-element.4) | data formatting | bytes 1327104
  133.4 1.1 copy.8

commit v2 on v1

v2 whole, which is shorter than its diff:
```python
import functools
import math

import jax
import jax.numpy as jnp
from jax import lax
from jax.experimental import pallas as pl
from jax.experimental.pallas import tpu as pltpu
from jax.sharding import PartitionSpec as P

D = 2304
F = 18432
SEQ = 256
MESH = pl.DeviceIdType.MESH
NZ = 8
SIDE = 4
OWN = 72
EX = 4
TOK = EX * SEQ
COLS = F // NZ
BOUND = math.sqrt(F * D * SEQ)
PIECES = ((0, 16, 1280), (16, 16, 1024), (32, 16, 1280), (48, 16, 1024), (64, 8, 1280))
TILE = 256
ORDER = (
    "g10 g21 a010 g20", "a011 x g31 a020", "g30 a021 g41 a030", "g40 a031 a040 a110", "G a041 a111 a210",
    "a120 n a211 l0", "X s0 m0002 a121", "m0024 a130 m0045 m0102", "a220 m0124 a131 a140", "a221 a141 a230 a310",
    "l1 s1 m1002 a231", "r00 a311 r01 m1024", "a240 m1102 a241 a320", "m1124 a321 m1145 a410", "l2 s2 a411 m2002",
    "a330 m2024 a331 m2045", "a420 m2102 a421 r10", "a340 m2124 a341 R00", "a430 R01 a431 r11", "l3 s3 m3002 a440",
    "a441 m3024 r20 m3102", "m3124 m3145 l4 s4", "r21 m4002 m4024 m4045", "m4102 m4124 R10 r30", "R11 R20 R21 r31",
    "r40 r41 R30 R31", "R40 R41",
)
F32, BF16 = jnp.float32, jnp.bfloat16


def nt_dot(a, b):
    return lax.dot_general(a, b, (((1,), (1,)), ((), ())), preferred_element_type=F32)


def kernel(x_hbm, g_hbm, out, clip_out, *scratch):
    NP = len(PIECES)
    names = iter(scratch)
    acts, graw, gt, clipv, tile, parts, gram, gram_s, gram_r = (next(names) for _ in range(9))
    grads = [next(names) for _ in PIECES]
    peer = [next(names) for _ in PIECES]
    scaled = [next(names) for _ in PIECES]
    part = [next(names) for _ in PIECES]
    send1 = [(next(names), next(names)) for _ in PIECES]
    recv1 = [(next(names), next(names)) for _ in PIECES]
    sums = [(next(names), next(names)) for _ in PIECES]
    recv2 = [(next(names), next(names)) for _ in PIECES]
    far_s = [(next(names), next(names)) for _ in PIECES]
    far_r = [(next(names), next(names)) for _ in PIECES]
    local_sem, gs_s, gs_r, pair_s, pair_r, ring_s, ring_r, norm_s, norm_r, p1_s, p1_r, p2_s, p2_r = names

    dp, z = lax.axis_index("dp"), lax.axis_index("mp")
    y, x, c = dp // 8, (dp // 2) % SIDE, dp % 2
    other = 1 - c

    def at(y, x, c, z):
        return (y * 8 + x * 2 + c, z)

    def xs(k):
        return lax.rem(x + k, SIDE)

    def ys(k):
        return lax.rem(y + k, SIDE)

    def zs(k):
        return lax.rem(z + k + NZ, NZ)

    peer_id = at(y, x, other, z)
    group = [(dz, dc) for dz in range(NZ) for dc in range(2) if dz or dc]

    def group_id(dz, dc):
        return at(y, x, lax.rem(c + dc, 2), zs(dz))

    load_x = pltpu.make_async_copy(x_hbm, acts.at[pl.ds(c * EX, EX)], local_sem.at[0])
    load_g = pltpu.make_async_copy(g_hbm, graw, local_sem.at[1])
    load_g.start()
    load_x.start()

    barrier = pltpu.get_barrier_semaphore()
    for dz, dc in group:
        pl.semaphore_signal(barrier, inc=1, device_id=group_id(dz, dc), device_id_type=MESH)
    for k in range(1, SIDE):
        pl.semaphore_signal(barrier, inc=1, device_id=at(y, xs(k), c, z), device_id_type=MESH)
        pl.semaphore_signal(barrier, inc=1, device_id=at(ys(k), x, c, z), device_id_type=MESH)

    def remote(src, dst, ssem, rsem, to):
        return pltpu.make_async_remote_copy(
            src_ref=src, dst_ref=dst, send_sem=ssem, recv_sem=rsem, device_id=to, device_id_type=MESH
        )

    begun, arrived = [], set()

    def start(copy, *key):
        copy(*key).start()
        begun.append((copy, key))

    def arrive(copy, *key):
        if (copy, key) not in arrived:
            arrived.add((copy, key))
            incoming.get(copy, copy)(*key).wait_recv()

    def pair_x():
        here = acts.at[pl.ds(c * EX, EX)]
        return remote(here, here, pair_s.at[0], pair_r.at[0], peer_id)


    token0 = pl.multiple_of(c * TOK, TOK)
    token1 = pl.multiple_of(other * TOK, TOK)

    def rows_of(core, first, n):
        return jnp.concatenate(
            [gt[pl.ds(pl.multiple_of(a * 2 * OWN + core * OWN + first, 8), n), :] for a in range(2)], axis=0
        ).astype(BF16)

    def pair_g(p):
        return remote(peer[p], grads[p].at[z, :, pl.ds(token0, TOK)], pair_s.at[1 + p], pair_r.at[1 + p], peer_id)

    def ring(p, s, h, q):
        src = zs(-(h - 1) if s == 0 else h - 1)
        view = grads[p].at[src, :, pl.ds(token0 if q == 0 else token1, TOK)]
        return remote(view, view, ring_s.at[p, s, h - 1, q], ring_r.at[p, s, h - 1, q],
                      at(y, x, c, zs(1 if s == 0 else -1)))

    def ring_in(p, s, h, q):
        src = zs(-h if s == 0 else h)
        view = grads[p].at[src, :, pl.ds(token0 if q == 0 else token1, TOK)]
        return remote(view, view, ring_s.at[p, s, h - 1, q], ring_r.at[p, s, h - 1, q],
                      at(y, x, c, zs(1 if s == 0 else -1)))

    def pair_g_in(p):
        view = grads[p].at[z, :, pl.ds(token1, TOK)]
        return remote(peer[p], view, pair_s.at[1 + p], pair_r.at[1 + p], peer_id)

    def ring_step(p, h, q):
        if h == 1 and q == 1:
            arrive(pair_g, p)
        for s in range(2):
            if h == 4 and s != q:
                arrive(ring, p, s, 3, q)
                continue
            if h > 1:
                arrive(ring, p, s, h - 1, q)
            start(ring, p, s, h, q)

    def ring_last(p):
        for s in range(2):
            arrive(ring, p, s, 4, s)

    def local_gram(e):
        for m, v in ((0, acts[c * EX + e]), (1, graw[e])):
            g = nt_dot(v, v)
            for d in range(NZ):
                side = 128 * (d // 4)
                gram[d, 2 * e + m, :32] = g[32 * d:32 * d + 32, side:side + 128]
                gram[d, 2 * e + m, 32:] = g[16 * d:16 * d + 16, 128:]

    def gram_copy(s, h, late):
        part = pl.ds((s ^ late) * EX, EX)
        return remote(gram_s.at[s, h - 1, part], gram_r.at[s, h - 1, part], gs_s.at[s, h - 1, late],
                      gs_r.at[s, h - 1, late], at(y, x, c, zs(1 if s == 0 else -1)))

    def gram_step(h, late):
        for s in range(2):
            d = zs(5 - h if s == 0 else h - 5)
            part = slice((s ^ late) * EX, ((s ^ late) + 1) * EX)
            v = gram[d, part]
            if h > 1 + late:
                arrive(gram_copy, s, h - 1, late)
                v = v + gram_r[s, h - 2, part].astype(F32)
            gram_s[s, h - 1, part] = v.astype(BF16)
            start(gram_copy, s, h, late)

    slot = z * 2 + c

    def gram_last():
        for s in range(2):
            arrive(gram_copy, s, 4, 1)
            arrive(gram_copy, s, 4, 0)
        v = gram[z] + gram_r[0, 3].astype(F32) + gram_r[1, 3].astype(F32)
        v = v.reshape(EX, 2, 48, 128)
        w = v[:, 0] * v[:, 1]
        tile[...] = jnp.sum(w[:, :32], axis=1) + 2.0 * jnp.sum(w[:, 32:], axis=1)
        parts[slot] = tile[...]
        for i in range(len(group)):
            start(norm, i)

    def norm(i):
        dz, dc = group[i]
        return remote(tile, parts.at[slot], norm_s.at[i], norm_r.at[i], group_id(dz, dc))

    def norm_in(i):
        dz, dc = group[i]
        src = lax.rem(z - dz + NZ, NZ) * 2 + lax.rem(c + dc, 2)
        return remote(tile, parts.at[src], norm_s.at[i], norm_r.at[i], group_id(dz, dc))

    def norm_wait():
        for i in range(len(group)):
            arrive(norm, i)
        for core in range(2):
            total = parts[core]
            for zz in range(1, NZ):
                total = total + parts[2 * zz + core]
            total = jnp.sum(total, axis=1, keepdims=True)
            factor = BOUND / jnp.maximum(jnp.sqrt(total), BOUND)
            for e in range(EX):
                b = core * EX + e
                clipv[:, b * SEQ:(b + 1) * SEQ] = jnp.broadcast_to(factor[e:e + 1, :], (1, SEQ))
        for e in range(EX):
            v = clipv[:, pl.ds(pl.multiple_of((c * EX + e) * SEQ, SEQ), 128)]
            clip_out[e] = jnp.max(v)

    def p1(p, half, k):
        to = at(y, xs(k), c, z) if half == 0 else at(ys(k), x, c, z)
        return remote(send1[p][half].at[k - 1], recv1[p][half].at[k - 1],
                      p1_s.at[p, half, k - 1], p1_r.at[p, half, k - 1], to)

    def p2(p, half, k):
        to = at(ys(k), x, c, z) if half == 0 else at(y, xs(k), c, z)
        block = ys(k) if half == 0 else xs(k)
        src, dst = (far_s[p][half], far_r[p][half]) if k == 2 else (sums[p][half].at[block], recv2[p][half].at[k // 2])
        return remote(src, dst, p2_s.at[p, half, k - 1], p2_r.at[p, half, k - 1], to)

    def span(p, half):
        cut = PIECES[p][2]
        return (0, cut) if half == 0 else (cut, COLS - cut)

    def dests(half, k):
        if half == 0:
            return [i * SIDE + xs(k) for i in range(SIDE)]
        return [ys(k) * SIDE + i for i in range(SIDE)]

    def scale(p):
        for zz in range(NZ):
            scaled[p][zz] = (grads[p][zz].astype(F32) * clipv[...]).astype(BF16)

    def multiply(p, half, lo, hi):
        first, n, _ = PIECES[p]
        base, width = span(p, half)

        def body(i, _):
            cols = pl.ds(pl.multiple_of(base + i * TILE, TILE), TILE)
            local = pl.ds(pl.multiple_of(i * TILE, TILE), TILE)
            lhs = scaled[p][...].reshape(NZ * 2 * n, 2 * TOK)
            rhs = acts[:, :, cols].reshape(2 * TOK, TILE)
            part[p][:, :, cols] = jnp.dot(lhs, rhs, preferred_element_type=F32).reshape(16, n, TILE)
            for k in range(1, SIDE):
                v = jnp.concatenate([part[p][j, :, cols] for j in dests(half, k)], axis=0)
                send1[p][half][k - 1, :, local] = v.astype(BF16)
            return 0

        lax.fori_loop(lo, min(hi, width // TILE), body, 0)
        if hi >= width // TILE:
            for k in range(1, SIDE):
                start(p1, p, half, k)

    def reduce1(p, half):
        first, n, _ = PIECES[p]
        base, width = span(p, half)
        for k in range(1, SIDE):
            arrive(p1, p, half, k)

        def body(i, _):
            cols = pl.ds(pl.multiple_of(base + i * TILE, TILE), TILE)
            local = pl.ds(pl.multiple_of(i * TILE, TILE), TILE)
            v = jnp.concatenate([part[p][j, :, cols] for j in dests(half, 0)], axis=0)
            for k in range(1, SIDE):
                v = v + recv1[p][half][k - 1, :, local].astype(F32)
            for i in range(SIDE):
                sums[p][half][i, :, local] = v[i * n:(i + 1) * n]
            return 0

        lax.fori_loop(0, width // TILE, body, 0)
        for k in (1, 3):
            start(p2, p, half, k)
        v = sums[p][half][ys(2) if half == 0 else xs(2)]
        far_s[p][half][...] = jnp.concatenate([v[:, :width // 2], v[:, width // 2:]], axis=0).astype(BF16)
        start(p2, p, half, 2)

    def reduce2(p, half):
        first, n, _ = PIECES[p]
        base, width = span(p, half)
        for k in range(1, SIDE):
            arrive(p2, p, half, k)
        v = sums[p][half][y if half == 0 else x] + recv2[p][half][0] + recv2[p][half][1]
        far = far_r[p][half][...].astype(F32)
        v = v + jnp.concatenate([far[:n], far[n:]], axis=1)
        out[first:first + n, base:base + width] = v * (1.0 / 128)

    def pair_x_in():
        return remote(x_hbm, acts.at[pl.ds(other * EX, EX)], pair_s.at[0], pair_r.at[0], peer_id)

    def wait_pair_x():
        arrive(pair_x)

    def begin_pair_x():
        start(pair_x)

    incoming = {pair_x: pair_x_in, pair_g: pair_g_in, ring: ring_in, norm: norm_in}

    load_g.wait()
    for e in range(EX):
        gt[:, e * SEQ:(e + 1) * SEQ] = graw[e].astype(F32).T
    for p, (first, n, _) in enumerate(PIECES):
        peer[p][...] = rows_of(other, first, n)
        grads[p][z, :, pl.ds(token0, TOK)] = rows_of(c, first, n)

    load_x.wait()
    for e in range(EX):
        local_gram(e)
    pl.semaphore_wait(barrier, len(group) + 2 * (SIDE - 1))
    for p in range(NP):
        start(pair_g, p)

    steps = {
        "a": ring_step,
        "l": ring_last,
        "g": gram_step,
        "G": gram_last,
        "n": norm_wait,
        "x": begin_pair_x,
        "X": wait_pair_x,
        "s": scale,
        "m": multiply,
        "r": reduce1,
        "R": reduce2,
    }
    for word in " ".join(ORDER).split():
        steps[word[0]](*(int(v) for v in word[1:]))

    for copy, key in begun:
        arrive(copy, *key)
        copy(*key).wait_send()


def on_device(acts, out_grads):
    np_ = len(PIECES)
    dma = pltpu.SemaphoreType.DMA
    scratch = [
        pltpu.VMEM((2 * EX, SEQ, COLS), BF16),
        pltpu.VMEM((EX, SEQ, D // NZ), BF16),
        pltpu.VMEM((D // NZ, TOK), F32),
        pltpu.VMEM((1, 2 * TOK), F32),
        pltpu.VMEM((EX, 128), F32),
        pltpu.VMEM((2 * NZ, EX, 128), F32),
        pltpu.VMEM((NZ, 2 * EX, 48, 128), F32),
        pltpu.VMEM((2, 4, 2 * EX, 48, 128), BF16),
        pltpu.VMEM((2, 4, 2 * EX, 48, 128), BF16),
    ]
    widths = [((0, cut), (1, COLS - cut)) for _, _, cut in PIECES]
    scratch += [pltpu.VMEM((NZ, 2 * n, 2 * TOK), BF16) for _, n, _ in PIECES]
    scratch += [pltpu.VMEM((2 * n, TOK), BF16) for _, n, _ in PIECES]
    scratch += [pltpu.VMEM((NZ, 2 * n, 2 * TOK), BF16) for _, n, _ in PIECES]
    scratch += [pltpu.VMEM((16, n, COLS), F32) for _, n, _ in PIECES]
    for shape in ("send", "recv"):
        scratch += [
            pltpu.VMEM((3, 4 * n, w), BF16) for (_, n, cut) in PIECES for w in (cut, COLS - cut)
        ]
    scratch += [pltpu.VMEM((4, n, w), F32) for (_, n, cut) in PIECES for w in (cut, COLS - cut)]
    scratch += [pltpu.VMEM((2, n, w), F32) for (_, n, cut) in PIECES for w in (cut, COLS - cut)]
    for shape in ("send", "recv"):
        scratch += [pltpu.VMEM((2 * n, w // 2), BF16) for (_, n, cut) in PIECES for w in (cut, COLS - cut)]
    scratch += [
        dma((2,)),
        dma((2, 4, 2)),
        dma((2, 4, 2)),
        dma((1 + np_,)),
        dma((1 + np_,)),
        dma((np_, 2, 4, 2)),
        dma((np_, 2, 4, 2)),
        dma((15,)),
        dma((15,)),
        dma((np_, 2, 3)),
        dma((np_, 2, 3)),
        dma((np_, 2, 3)),
        dma((np_, 2, 3)),
    ]
    return pl.pallas_call(
        kernel,
        out_shape=(
            jax.ShapeDtypeStruct((OWN, COLS), F32),
            jax.ShapeDtypeStruct((EX,), F32),
        ),
        in_specs=[pl.BlockSpec(memory_space=pl.ANY)] * 2,
        out_specs=(pl.BlockSpec(memory_space=pltpu.VMEM), pl.BlockSpec(memory_space=pltpu.SMEM)),
        scratch_shapes=scratch,
        compiler_params=pltpu.CompilerParams(
            collective_id=0, has_side_effects=True, vmem_limit_bytes=60 * 2**20
        ),
        name="clipped_grad",
    )(acts, out_grads)


def solution(mesh):
    in_specs = (P("dp", None, "mp"), P("dp", None, "mp"))
    out_specs = (P("dp", "mp"), P("dp"))
    return jax.shard_map(
        on_device, mesh=mesh, in_specs=in_specs, out_specs=out_specs, check_vma=False
    )
```

time: 135 us -> 98.7 us (0.73)
  Pallas kernels: 129 us -> 92.5 us
    pallas_call x1, Pallas kernels: 129 us -> 92.5 us  [on_device(): pl.pallas_call(kernel, out_shape=(jax.ShapeDtypeStruct((OWN, COLS), F32),...]
where the time goes in v2:
time: 98.7 us; the launch traced here: 98.5 us
  Pallas kernels  92.5 us (94%)
  local copies, waits for them, and re-layouts  5.32 us (5%)
    pallas_call x1, Pallas kernels, on_device(): pl.pallas_call(kernel, out_shape=(jax.ShapeDtypeStruct((OWN, COLS), F32),...  92.5 us
    unnamed x3, local copies, waits for them, and re-layouts  5.32 us

profile of v2, /device:TPU:2, one launch (start us, length us, event | category | flops | bytes accessed | tf_op | source)
XLA Modules:
  0.0 98.5 jit_solution(17383182761755654292)
XLA Ops:
  0.6 2.2 %copy.4.g_hbm = bf16[4,256,288]{2,1,0:T(8,128)(2,1)} copy(bf16[4,256,288]{1,2,0:T(8,128)(2,1)} %param.3) | data formatting | bytes 1179648 | tf_op args[1]
  2.9 92.5 %clipped_grad.1 = (f32[72,2304]{1,0:T(8,128)}, f32[4]{0:T(128)}) custom-call(bf16[4,256,2304]{2,1,0:T(8,128)(2,1)} %x_hbm.1, bf16[4,256,288]{2,1,0:T(8,128)(2,1)} %copy.4.g_hbm), custom_call_target="tpu_custom_call" | custom-call | tf_op jit(solution)/shard_map/clipped_grad/pallas_call | solution.py:380
  95.3 2.0 %copy.7 = f32[72,2304]{1,0:T(8,128)} copy(f32[72,2304]{1,0:T(8,128)} %get-tuple-element.4) | data formatting | bytes 1327104
  97.3 1.1 %copy.8 = f32[4]{0:T(128)} copy(f32[4]{0:T(128)} %get-tuple-element.5) | data formatting | bytes 32

commit v3 on v2

--- a/solution.py
+++ b/solution.py
@@ -32,11 +32,15 @@
 F32, BF16 = jnp.float32, jnp.bfloat16
 
 
+def tn_dot(a, b):
+    return lax.dot_general(a, b, (((0,), (0,)), ((), ())), preferred_element_type=F32)
+
+
 def nt_dot(a, b):
     return lax.dot_general(a, b, (((1,), (1,)), ((), ())), preferred_element_type=F32)
 
 
-def kernel(x_hbm, g_hbm, out, clip_out, *scratch):
+def kernel(x_hbm, g_hbm, out_hbm, clip_out, *scratch):
     NP = len(PIECES)
     names = iter(scratch)
     acts, graw, gt, clipv, tile, parts, gram, gram_s, gram_r = (next(names) for _ in range(9))
@@ -50,7 +54,7 @@
     recv2 = [(next(names), next(names)) for _ in PIECES]
     far_s = [(next(names), next(names)) for _ in PIECES]
     far_r = [(next(names), next(names)) for _ in PIECES]
-    local_sem, gs_s, gs_r, pair_s, pair_r, ring_s, ring_r, norm_s, norm_r, p1_s, p1_r, p2_s, p2_r = names
+    out, local_sem, out_sem, gs_s, gs_r, pair_s, pair_r, ring_s, ring_r, norm_s, norm_r, p1_s, p1_r, p2_s, p2_r = names
 
     dp, z = lax.axis_index("dp"), lax.axis_index("mp")
     y, x, c = dp // 8, (dp // 2) % SIDE, dp % 2
@@ -150,8 +154,8 @@
             arrive(ring, p, s, 4, s)
 
     def local_gram(e):
-        for m, v in ((0, acts[c * EX + e]), (1, graw[e])):
-            g = nt_dot(v, v)
+        v = acts[c * EX + e]
+        for m, g in ((0, nt_dot(v, v)), (1, tn_dot(graw[e], graw[e]))):
             for d in range(NZ):
                 side = 128 * (d // 4)
                 gram[d, 2 * e + m, :32] = g[32 * d:32 * d + 32, side:side + 128]
@@ -279,6 +283,14 @@
         far_s[p][half][...] = jnp.concatenate([v[:, :width // 2], v[:, width // 2:]], axis=0).astype(BF16)
         start(p2, p, half, 2)
 
+    stored = []
+
+    def store(p, half):
+        first, n, _ = PIECES[p]
+        base, width = span(p, half)
+        view = (pl.ds(first, n), pl.ds(base, width))
+        return pltpu.make_async_copy(out.at[view], out_hbm.at[view], out_sem.at[p, half])
+
     def reduce2(p, half):
         first, n, _ = PIECES[p]
         base, width = span(p, half)
@@ -288,6 +300,8 @@
         far = far_r[p][half][...].astype(F32)
         v = v + jnp.concatenate([far[:n], far[n:]], axis=1)
         out[first:first + n, base:base + width] = v * (1.0 / 128)
+        store(p, half).start()
+        stored.append((p, half))
 
     def pair_x_in():
         return remote(x_hbm, acts.at[pl.ds(other * EX, EX)], pair_s.at[0], pair_r.at[0], peer_id)
@@ -302,7 +316,7 @@
 
     load_g.wait()
     for e in range(EX):
-        gt[:, e * SEQ:(e + 1) * SEQ] = graw[e].astype(F32).T
+        gt[:, e * SEQ:(e + 1) * SEQ] = graw[e].astype(F32)
     for p, (first, n, _) in enumerate(PIECES):
         peer[p][...] = rows_of(other, first, n)
         grads[p][z, :, pl.ds(token0, TOK)] = rows_of(c, first, n)
@@ -330,9 +344,17 @@
     for word in " ".join(ORDER).split():
         steps[word[0]](*(int(v) for v in word[1:]))
 
+    for key in stored:
+        store(*key).wait()
     for copy, key in begun:
         arrive(copy, *key)
         copy(*key).wait_send()
+
+
+def hand_on(total, factor, out, clip_out):
+    out[...] = total[...]
+    for e in range(EX):
+        clip_out[e] = factor[e]
 
 
 def on_device(acts, out_grads):
@@ -340,7 +362,7 @@
     dma = pltpu.SemaphoreType.DMA
     scratch = [
         pltpu.VMEM((2 * EX, SEQ, COLS), BF16),
-        pltpu.VMEM((EX, SEQ, D // NZ), BF16),
+        pltpu.VMEM((EX, D // NZ, SEQ), BF16),
         pltpu.VMEM((D // NZ, TOK), F32),
         pltpu.VMEM((1, 2 * TOK), F32),
         pltpu.VMEM((EX, 128), F32),
@@ -363,7 +385,9 @@
     for shape in ("send", "recv"):
         scratch += [pltpu.VMEM((2 * n, w // 2), BF16) for (_, n, cut) in PIECES for w in (cut, COLS - cut)]
     scratch += [
+        pltpu.VMEM((OWN, COLS), F32),
         dma((2,)),
+        dma((np_, 2)),
         dma((2, 4, 2)),
         dma((2, 4, 2)),
         dma((1 + np_,)),
@@ -377,20 +401,30 @@
         dma((np_, 2, 3)),
         dma((np_, 2, 3)),
     ]
-    return pl.pallas_call(
+    total, factor = pl.pallas_call(
         kernel,
         out_shape=(
             jax.ShapeDtypeStruct((OWN, COLS), F32),
             jax.ShapeDtypeStruct((EX,), F32),
         ),
         in_specs=[pl.BlockSpec(memory_space=pl.ANY)] * 2,
-        out_specs=(pl.BlockSpec(memory_space=pltpu.VMEM), pl.BlockSpec(memory_space=pltpu.SMEM)),
+        out_specs=(pl.BlockSpec(memory_space=pl.ANY), pl.BlockSpec(memory_space=pltpu.SMEM)),
         scratch_shapes=scratch,
         compiler_params=pltpu.CompilerParams(
             collective_id=0, has_side_effects=True, vmem_limit_bytes=60 * 2**20
         ),
         name="clipped_grad",
-    )(acts, out_grads)
+    )(acts, jnp.swapaxes(out_grads, 1, 2))
+    return pl.pallas_call(
+        hand_on,
+        out_shape=(
+            jax.ShapeDtypeStruct((OWN, COLS), F32),
+            jax.ShapeDtypeStruct((EX,), F32),
+        ),
+        in_specs=[pl.BlockSpec(memory_space=pltpu.VMEM), pl.BlockSpec(memory_space=pltpu.SMEM)],
+        out_specs=(pl.BlockSpec(memory_space=pltpu.VMEM), pl.BlockSpec(memory_space=pltpu.SMEM)),
+        name="hand_on",
+    )(total, factor)
 
 
 def solution(mesh):

time: 98.7 us -> 96.6 us (0.979)
  local copies, waits for them, and re-layouts: 5.32 us -> 0 us
  Pallas kernels: 92.5 us -> 95.6 us
    unnamed x3 -> x0, local copies, waits for them, and re-layouts: 5.32 us -> none
    pallas_call x0 -> x1, Pallas kernels: none -> 1.99 us  [on_device(): pl.pallas_call(hand_on, out_shape=(jax.ShapeDtypeStruct((OWN, COLS), F32)...]
    pallas_call x1, Pallas kernels: 92.5 us -> 93.6 us  [on_device(): pl.pallas_call(kernel, out_shape=(jax.ShapeDtypeStruct((OWN, COLS), F32),...]
where the time goes in v3:
time: 96.6 us; the launch traced here: 96.4 us
  Pallas kernels  95.6 us (99%)
    pallas_call x1, Pallas kernels, on_device(): pl.pallas_call(kernel, out_shape=(jax.ShapeDtypeStruct((OWN, COLS), F32),...  93.6 us
    pallas_call x1, Pallas kernels, on_device(): pl.pallas_call(hand_on, out_shape=(jax.ShapeDtypeStruct((OWN, COLS), F32)...  1.99 us

profile of v3, /device:TPU:2, one launch (start us, length us, event | category | flops | bytes accessed | tf_op | source)
XLA Modules:
  0.0 96.4 jit_solution(12012621283819869721)
XLA Ops:
  0.6 93.6 %clipped_grad.1 = (f32[72,2304]{1,0:T(8,128)}, f32[4]{0:T(128)}) custom-call(bf16[4,256,2304]{2,1,0:T(8,128)(2,1)} %x_hbm.1, bf16[4,288,256]{2,1,0:T(8,128)(2,1)} %bitcast.1), custom_call_target="tpu_custom_call" | custom-call | tf_op jit(solution)/shard_map/clipped_grad/pallas_call | solution.py:404
  94.3 2.0 %hand_on.1 = (f32[72,2304]{1,0:T(8,128)}, f32[4]{0:T(128)}) custom-call(f32[72,2304]{1,0:T(8,128)} %get-tuple-element.4.total, f32[4]{0:T(128)} %get-tuple-element.5.factor), custom_call_target="tpu_custom_call" | custom-call | tf_op jit(solution)/shard_map/hand_on/pallas_call | solution.py:418

commit v4 on v3

--- a/solution.py
+++ b/solution.py
@@ -21,13 +21,15 @@
 BOUND = math.sqrt(F * D * SEQ)
 PIECES = ((0, 16, 1280), (16, 16, 1024), (32, 16, 1280), (48, 16, 1024), (64, 8, 1280))
 TILE = 256
+HALF = 160
 ORDER = (
-    "g10 g21 a010 g20", "a011 x g31 a020", "g30 a021 g41 a030", "g40 a031 a040 a110", "G a041 a111 a210",
-    "a120 n a211 l0", "X s0 m0002 a121", "m0024 a130 m0045 m0102", "a220 m0124 a131 a140", "a221 a141 a230 a310",
-    "l1 s1 m1002 a231", "r00 a311 r01 m1024", "a240 m1102 a241 a320", "m1124 a321 m1145 a410", "l2 s2 a411 m2002",
-    "a330 m2024 a331 m2045", "a420 m2102 a421 r10", "a340 m2124 a341 R00", "a430 R01 a431 r11", "l3 s3 m3002 a440",
-    "a441 m3024 r20 m3102", "m3124 m3145 l4 s4", "r21 m4002 m4024 m4045", "m4102 m4124 R10 r30", "R11 R20 R21 r31",
-    "r40 r41 R30 R31", "R40 R41",
+    "g10 g21 a010 g20", "a011 x a110 g31", "g30 a020 a021 a111", "g41 g40 a030 a031", "a120 G a040 a041",
+    "a121 a130 n a210", "l0 X s0 a211", "m0001 m0012 m0023 a131", "m0034 m0045 a140 m0101", "m0112 a220 m0123 m0134",
+    "a141 a221 a310 l1", "s1 m1001 a311 m1012", "m1023 a230 m1034 m1101", "m1112 a231 m1123 r00", "a320 r01 a321 m1134",
+    "m1145 a240 a241 a330", "R00 a410 r10 a331", "l2 s2 a411 m2001", "m2012 a340 m2023 m2034", "a420 m2045 m2101 a341",
+    "a421 r11 m2112 m2123", "m2134 a430 l3 s3", "m3001 m3012 a431 m3023", "m3034 m3101 m3112 a440", "m3123 m3134 m3145 a441",
+    "R01 R10 r20 l4", "s4 m4001 r21 m4012", "m4023 m4034 m4045 m4101", "m4112 m4123 m4134 R11", "r30 r31 R21 R20",
+    "r40 r41 R31 R30", "R40 R41",
 )
 F32, BF16 = jnp.float32, jnp.bfloat16
 
@@ -156,20 +158,23 @@
     def local_gram(e):
         v = acts[c * EX + e]
         for m, g in ((0, nt_dot(v, v)), (1, tn_dot(graw[e], graw[e]))):
-            for d in range(NZ):
-                side = 128 * (d // 4)
-                gram[d, 2 * e + m, :32] = g[32 * d:32 * d + 32, side:side + 128]
-                gram[d, 2 * e + m, 32:] = g[16 * d:16 * d + 16, 128:]
+            blocks = [g[64 * i:64 * i + 64, 64 * i:64 * i + 128] for i in range(3)]
+            blocks.append(jnp.concatenate([g[192:, 192:], g[192:, :64]], axis=1))
+            blocks.append(jnp.concatenate([g[:64, 128:192], g[64:128, 192:]], axis=1))
+            for i, block in enumerate(blocks):
+                row = (2 * e + m) * 40 + 8 * i
+                for d in range(NZ):
+                    gram[d, row:row + 8] = block[8 * d:8 * d + 8]
 
     def gram_copy(s, h, late):
-        part = pl.ds((s ^ late) * EX, EX)
+        part = pl.ds((s ^ late) * HALF, HALF)
         return remote(gram_s.at[s, h - 1, part], gram_r.at[s, h - 1, part], gs_s.at[s, h - 1, late],
                       gs_r.at[s, h - 1, late], at(y, x, c, zs(1 if s == 0 else -1)))
 
     def gram_step(h, late):
         for s in range(2):
             d = zs(5 - h if s == 0 else h - 5)
-            part = slice((s ^ late) * EX, ((s ^ late) + 1) * EX)
+            part = slice((s ^ late) * HALF, ((s ^ late) + 1) * HALF)
             v = gram[d, part]
             if h > 1 + late:
                 arrive(gram_copy, s, h - 1, late)
@@ -184,9 +189,10 @@
             arrive(gram_copy, s, 4, 1)
             arrive(gram_copy, s, 4, 0)
         v = gram[z] + gram_r[0, 3].astype(F32) + gram_r[1, 3].astype(F32)
-        v = v.reshape(EX, 2, 48, 128)
+        v = v.reshape(EX, 2, 40, 128)
         w = v[:, 0] * v[:, 1]
-        tile[...] = jnp.sum(w[:, :32], axis=1) + 2.0 * jnp.sum(w[:, 32:], axis=1)
+        twice = 1.0 + (lax.broadcasted_iota(jnp.int32, (EX, 128), 1) >= 64).astype(F32)
+        tile[...] = twice * jnp.sum(w[:, :32], axis=1) + 2.0 * jnp.sum(w[:, 32:], axis=1)
         parts[slot] = tile[...]
         for i in range(len(group)):
             start(norm, i)
@@ -367,9 +373,9 @@
         pltpu.VMEM((1, 2 * TOK), F32),
         pltpu.VMEM((EX, 128), F32),
         pltpu.VMEM((2 * NZ, EX, 128), F32),
-        pltpu.VMEM((NZ, 2 * EX, 48, 128), F32),
-        pltpu.VMEM((2, 4, 2 * EX, 48, 128), BF16),
-        pltpu.VMEM((2, 4, 2 * EX, 48, 128), BF16),
+        pltpu.VMEM((NZ, 2 * HALF, 128), F32),
+        pltpu.VMEM((2, 4, 2 * HALF, 128), BF16),
+        pltpu.VMEM((2, 4, 2 * HALF, 128), BF16),
     ]
     widths = [((0, cut), (1, COLS - cut)) for _, _, cut in PIECES]
     scratch += [pltpu.VMEM((NZ, 2 * n, 2 * TOK), BF16) for _, n, _ in PIECES]

time: 96.6 us -> 94.8 us (0.981)
  Pallas kernels: 95.6 us -> 93.9 us
    pallas_call x1, Pallas kernels: 93.6 us -> 91.9 us  [on_device(): pl.pallas_call(kernel, out_shape=(jax.ShapeDtypeStruct((OWN, COLS), F32),...]
where the time goes in v4:
time: 94.8 us; the launch traced here: 94.7 us
  Pallas kernels  93.9 us (99%)
    pallas_call x1, Pallas kernels, on_device(): pl.pallas_call(kernel, out_shape=(jax.ShapeDtypeStruct((OWN, COLS), F32),...  91.9 us
    pallas_call x1, Pallas kernels, on_device(): pl.pallas_call(hand_on, out_shape=(jax.ShapeDtypeStruct((OWN, COLS), F32)...  1.99 us

profile of v4, /device:TPU:2, one launch (start us, length us, event | category | flops | bytes accessed | tf_op | source)
XLA Modules:
  0.0 94.7 jit_solution(173860526459327687)
XLA Ops:
  0.6 91.9 %clipped_grad.1 = (f32[72,2304]{1,0:T(8,128)}, f32[4]{0:T(128)}) custom-call(bf16[4,256,2304]{2,1,0:T(8,128)(2,1)} %x_hbm.1, bf16[4,288,256]{2,1,0:T(8,128)(2,1)} %bitcast.1), custom_call_target="tpu_custom_call" | custom-call | tf_op jit(solution)/shard_map/clipped_grad/pallas_call | solution.py:410
  92.5 2.0 %hand_on.1 = (f32[72,2304]{1,0:T(8,128)}, f32[4]{0:T(128)}) custom-call(f32[72,2304]{1,0:T(8,128)} %get-tuple-element.4.total, f32[4]{0:T(128)} %get-tuple-element.5.factor), custom_call_target="tpu_custom_call" | custom-call | tf_op jit(solution)/shard_map/hand_on/pallas_call | solution.py:424

commit v5 on v4

--- a/solution.py
+++ b/solution.py
@@ -25,11 +25,11 @@
 ORDER = (
     "g10 g21 a010 g20", "a011 x a110 g31", "g30 a020 a021 a111", "g41 g40 a030 a031", "a120 G a040 a041",
     "a121 a130 n a210", "l0 X s0 a211", "m0001 m0012 m0023 a131", "m0034 m0045 a140 m0101", "m0112 a220 m0123 m0134",
-    "a141 a221 a310 l1", "s1 m1001 a311 m1012", "m1023 a230 m1034 m1101", "m1112 a231 m1123 r00", "a320 r01 a321 m1134",
-    "m1145 a240 a241 a330", "R00 a410 r10 a331", "l2 s2 a411 m2001", "m2012 a340 m2023 m2034", "a420 m2045 m2101 a341",
-    "a421 r11 m2112 m2123", "m2134 a430 l3 s3", "m3001 m3012 a431 m3023", "m3034 m3101 m3112 a440", "m3123 m3134 m3145 a441",
-    "R01 R10 r20 l4", "s4 m4001 r21 m4012", "m4023 m4034 m4045 m4101", "m4112 m4123 m4134 R11", "r30 r31 R21 R20",
-    "r40 r41 R31 R30", "R40 R41",
+    "a141 a221 a310 l1", "s1 m1001 a311 m1012", "m1023 a230 m1034 m1101", "m1112 a231 m1123 m1134", "a320 m1145 r00 a321",
+    "r01 a240 a241 a330", "a410 r10 a331 l2", "s2 a411 m2001 m2012", "a340 m2023 m2034 a420", "m2045 m2101 a341 a421",
+    "m2112 m2123 m2134 l3", "s3 m3001 a430 m3012", "m3023 a431 m3034 m3101", "m3112 m3123 m3134 a440", "m3145 r11 a441 R00",
+    "R01 r20 R10 r21", "l4 s4 m4001 m4012", "m4023 m4034 m4045 m4101", "m4112 m4123 m4134 r30", "R11 r31 R21 R20",
+    "r41 r40 R30 R31", "R41 R40",
 )
 F32, BF16 = jnp.float32, jnp.bfloat16
 
@@ -357,10 +357,21 @@
         copy(*key).wait_send()
 
 
-def hand_on(total, factor, out, clip_out):
-    out[...] = total[...]
+def hand_on(total, factor, out, clip_out, held, sems):
+    def copy(way, i):
+        rows = pl.ds(24 * i, 24)
+        src, dst = ((total, held), (held, out))[way]
+        return pltpu.make_async_copy(src.at[rows], dst.at[rows], sems.at[way, i])
+
+    for i in range(3):
+        copy(0, i).start()
     for e in range(EX):
         clip_out[e] = factor[e]
+    for i in range(3):
+        copy(0, i).wait()
+        copy(1, i).start()
+    for i in range(3):
+        copy(1, i).wait()
 
 
 def on_device(acts, out_grads):
@@ -427,8 +438,9 @@
             jax.ShapeDtypeStruct((OWN, COLS), F32),
             jax.ShapeDtypeStruct((EX,), F32),
         ),
-        in_specs=[pl.BlockSpec(memory_space=pltpu.VMEM), pl.BlockSpec(memory_space=pltpu.SMEM)],
-        out_specs=(pl.BlockSpec(memory_space=pltpu.VMEM), pl.BlockSpec(memory_space=pltpu.SMEM)),
+        in_specs=[pl.BlockSpec(memory_space=pl.ANY), pl.BlockSpec(memory_space=pltpu.SMEM)],
+        out_specs=(pl.BlockSpec(memory_space=pl.ANY), pl.BlockSpec(memory_space=pltpu.SMEM)),
+        scratch_shapes=[pltpu.VMEM((OWN, COLS), F32), dma((2, 3))],
         name="hand_on",
     )(total, factor)
 

time: 94.8 us -> 95.9 us (1.012)
  Pallas kernels: 93.9 us -> 94.9 us
    pallas_call x1, Pallas kernels: 1.99 us -> 3.06 us  [on_device(): pl.pallas_call(hand_on, out_shape=(jax.ShapeDtypeStruct((OWN, COLS), F32)...]
where the time goes in v5:
time: 95.9 us; the launch traced here: 95.7 us
  Pallas kernels  94.9 us (99%)
    pallas_call x1, Pallas kernels, on_device(): pl.pallas_call(kernel, out_shape=(jax.ShapeDtypeStruct((OWN, COLS), F32),...  91.9 us
    pallas_call x1, Pallas kernels, on_device(): pl.pallas_call(hand_on, out_shape=(jax.ShapeDtypeStruct((OWN, COLS), F32)...  3.06 us

profile of v5, /device:TPU:2, one launch (start us, length us, event | category | flops | bytes accessed | tf_op | source)
XLA Modules:
  0.0 95.7 jit_solution(1640052767118709773)
XLA Ops:
  0.6 91.9 %clipped_grad.1 = (f32[72,2304]{1,0:T(8,128)}, f32[4]{0:T(128)}) custom-call(bf16[4,256,2304]{2,1,0:T(8,128)(2,1)} %x_hbm.1, bf16[4,288,256]{2,1,0:T(8,128)(2,1)} %bitcast.1), custom_call_target="tpu_custom_call" | custom-call | tf_op jit(solution)/shard_map/clipped_grad/pallas_call | solution.py:421
  92.5 3.1 %hand_on.1 = (f32[72,2304]{1,0:T(8,128)}, f32[4]{0:T(128)}) custom-call(f32[72,2304]{1,0:T(8,128)} %get-tuple-element.4.total, f32[4]{0:T(128)} %get-tuple-element.5.factor), custom_call_target="tpu_custom_call" | custom-call | tf_op jit(solution)/shard_map/hand_on/pallas_call | solution.py:435
